TPU v7x, 32 devices: a whole 2x2x4 slice. The times are simulated.
32 devices in a mesh: section: 4 (over x, core), ep: 8 (over z, y).
Axes of the slice: x: 2, y: 2, z: 4, core: 2. Of those that a mesh axis runs over, the one named last changes fastest.
Arguments:
- tokens: bfloat16 [4, 1024, 4096], P('section', 'ep'), may hold values from -6 to 6
- routes: int32 [4, 1024, 8], P('section', 'ep'), may hold values from 0 to 127, as said below
- router_weights: float32 [4, 1024, 8], P('section', 'ep'), may hold values from 0.25 to 1
- w_gate: bfloat16 [4, 8, 4096, 384], P('section', 'ep'), may hold values from -0.09375 to 0.09375
- w_up: bfloat16 [4, 8, 4096, 384], P('section', 'ep'), may hold values from -0.09375 to 0.09375
- w_down: bfloat16 [4, 8, 384, 4096], P('section', 'ep'), may hold values from -0.15625 to 0.15625
- w_query: bfloat16 [4, 4096, 1024], P('section', 'ep'), may hold values from -0.09375 to 0.09375
- w_keyval: bfloat16 [4, 4096, 256], P('section', 'ep'), may hold values from -0.09375 to 0.09375
- gain_query: float32 [4, 128], P('section'), may hold values from 0.8 to 2
- gain_key: float32 [4, 128], P('section'), may hold values from 0.8 to 2
- segment_ids: int32 [4, 1024], P('section', 'ep'), may hold values from 0 to 3, never falling along the last dimension, each value on 1 to 512 neighbouring positions
Outputs:
- layer_out: bfloat16 [4, 1024, 4096], P('section', 'ep')
- attended: bfloat16 [4, 1024, 1024], P('section', 'ep')
Inputs may be any that keep to these rules, and one draw needn't show every extreme that they name: `routes`: each token names 8 different experts, at most one of them below 2. Among the tokens of one device (aligned blocks of 128 rows in each section) no expert below 2 is named by more than 64 of them, and in each section one expert below 2 is named by exactly 64 tokens of every block. `segment_ids`: along each section's tokens the reaction numbers never fall; each reaction spans 1 to 512 tokens and one spans exactly 512.
All inputs are finite; a program needn't handle non-finite values.
Results may differ from a plain program's by a relative error of at most 0.018.
Values may be sent and summed in bfloat16 or wider, within the bound.
A program may use at most 128 MiB of HBM per device.

v0:
```python
import math

import jax
import jax.numpy as jnp
from jax import lax
from jax.sharding import PartitionSpec as P

OWNERS = 4
SEG_MOST = 512


EPSILON = 1e-06
ROPE_BASE = 1000000.0
FAR_INDEX = 1073741824


def passed_along(block, axis, distance):
    devices = range(lax.axis_size(axis))
    route = [((i - distance) % len(devices), i) for i in devices]
    return lax.ppermute(block, axis, route)


def prefix(shard, axis, combine, identity):
    length, mine = (lax.axis_size(axis), lax.axis_index(axis))
    everything = jax.tree.map(lambda part: lax.all_gather(part, axis), shard)
    start = jax.tree.map(
        lambda part, zero: jnp.broadcast_to(jnp.asarray(zero, part.dtype), part.shape),
        shard,
        identity,
    )

    def step(k, before):
        reached = k < mine
        new = combine(before, jax.tree.map(lambda part: part[k], everything))
        return jax.tree.map(lambda a, b: jnp.where(reached, a, b), new, before)

    return lax.fori_loop(0, length, step, start)


def passed_along_2(value, axis, steps):
    count = lax.axis_size(axis)
    leading, last = (max(0, -steps), min(count, count - steps))
    return lax.ppermute(value, axis, [(source, source + steps) for source in range(leading, last)])


def rms_rows(values):
    return values * lax.rsqrt(jnp.mean(values * values, axis=-1, keepdims=True) + EPSILON)


def rotary(values, position):
    half_count = values.shape[-1] // 2
    frequency = ROPE_BASE ** (-(jnp.arange(half_count, dtype=jnp.float32) * 2.0) / values.shape[-1])
    angles = position.astype(jnp.float32)[:, None] * frequency[None, :]
    cosine = jnp.concatenate([jnp.cos(angles), jnp.cos(angles)], axis=-1)[:, None, :]
    sine = jnp.concatenate([jnp.sin(angles), jnp.sin(angles)], axis=-1)[:, None, :]
    turned = jnp.concatenate([-values[..., half_count:], values[..., :half_count]], axis=-1)
    return values * cosine + turned * sine


def feed_forward(row_block, gate_part, up_part, down_part):
    gate_proj = jnp.dot(row_block, gate_part, preferred_element_type=jnp.float32)
    up_proj = jnp.dot(row_block, up_part, preferred_element_type=jnp.float32)
    activated = (jax.nn.silu(gate_proj) * up_proj).astype(jnp.bfloat16)
    return jnp.dot(activated, down_part, preferred_element_type=jnp.float32)


def keep_later(earlier, later):
    same_id = earlier[0] == later[0]
    newer_id = later[0] > earlier[0]
    start_at = jnp.where(
        same_id, jnp.minimum(earlier[1], later[1]), jnp.where(newer_id, later[1], earlier[1])
    )
    return (jnp.maximum(earlier[0], later[0]), start_at)


def on_device(
    tokens,
    routes,
    router_weights,
    w_gate,
    w_up,
    w_down,
    w_query,
    w_keyval,
    gain_query,
    gain_key,
    segment_ids,
):
    device_count = lax.axis_size("ep")
    expert_count = device_count // OWNERS
    token_count = tokens.shape[1]
    model_width = tokens.shape[2]
    capacity = OWNERS * max(1, token_count // device_count)
    wide_tokens = tokens[0].astype(jnp.float32)
    normed = rms_rows(wide_tokens).astype(jnp.bfloat16)
    inside = routes[0] < expert_count
    has_route = jnp.any(inside, axis=-1)
    chosen = jnp.sum(jnp.where(inside, routes[0], 0), axis=-1)
    weight_kept = jnp.sum(jnp.where(inside, router_weights[0], 0.0), axis=-1)
    expert_ids = jnp.arange(expert_count, dtype=jnp.int32)
    member = ((chosen[:, None] == expert_ids[None, :]) & has_route[:, None]).astype(jnp.int32)
    rank_within = jnp.sum((jnp.cumsum(member, axis=0) - member) * member, axis=-1)
    slot_index = jnp.where(has_route, chosen * capacity + rank_within, -1)
    slot_ids = jnp.arange(expert_count * capacity, dtype=jnp.int32)
    placing = (slot_ids[:, None] == slot_index[None, :]).astype(jnp.bfloat16)
    packed = jnp.dot(placing, normed, preferred_element_type=jnp.float32).astype(jnp.bfloat16)
    gate_part = w_gate[0, 0]
    up_part = w_up[0, 0]
    down_part = w_down[0, 0]
    spread = jnp.broadcast_to(
        packed.reshape(expert_count, 1, capacity, model_width),
        (expert_count, OWNERS, capacity, model_width),
    ).reshape(device_count, capacity, model_width)
    received = lax.all_to_all(spread, "ep", split_axis=0, concat_axis=0, tiled=True)
    partial_out = feed_forward(
        received.reshape(-1, model_width), gate_part, up_part, down_part
    ).reshape(received.shape)
    returned_rows = lax.all_to_all(
        partial_out.astype(jnp.bfloat16), "ep", split_axis=0, concat_axis=0, tiled=True
    ).astype(partial_out.dtype)
    merged = jnp.sum(
        returned_rows.reshape(expert_count, OWNERS, capacity, model_width), axis=1
    ).reshape(expert_count * capacity, model_width)
    fetched_rows = jnp.take(merged, jnp.maximum(slot_index, 0), axis=0)
    expert_out = jnp.where(has_route[:, None], fetched_rows, 0.0)
    layer_out = (wide_tokens + weight_kept[:, None] * expert_out).astype(jnp.bfloat16)
    arrived = passed_along(layer_out, "section", 1)
    lifted = rms_rows(arrived.astype(jnp.float32)).astype(jnp.bfloat16)
    head_dim = gain_query.shape[-1]
    query_width = w_query.shape[-1]
    head_count = query_width // head_dim
    query_raw = jnp.dot(
        lifted,
        lax.all_gather(w_query[0], "ep", axis=0, tiled=True),
        preferred_element_type=jnp.float32,
    )
    keyval_raw = jnp.dot(
        lifted,
        lax.all_gather(w_keyval[0], "ep", axis=0, tiled=True),
        preferred_element_type=jnp.float32,
    )
    segment_row = segment_ids[0]
    first_index = lax.axis_index("ep") * token_count
    global_index = first_index + jnp.arange(token_count, dtype=jnp.int32)
    change = jnp.concatenate([jnp.ones((1,), dtype=bool), segment_row[1:] != segment_row[:-1]])
    local_start = lax.cummax(jnp.where(change, global_index, 0), axis=0)
    empty_prior = (jnp.full((1,), -1, jnp.int32), jnp.full((1,), FAR_INDEX, jnp.int32))
    prior_id, prior_start = prefix(
        (segment_row[-1:], local_start[-1:]), "ep", keep_later, empty_prior
    )
    start_index = jnp.where(segment_row == prior_id[0], prior_start[0], local_start).astype(
        jnp.int32
    )
    position = global_index - start_index
    query = rotary(
        rms_rows(query_raw.reshape(token_count, head_count, head_dim)) * gain_query[0], position
    ).astype(jnp.bfloat16)
    key_part = rotary(rms_rows(keyval_raw[:, None, :head_dim]) * gain_key[0], position)[
        :, 0
    ].astype(jnp.bfloat16)
    value_part = keyval_raw[:, head_dim:].astype(jnp.bfloat16)
    key_value = jnp.concatenate([key_part, value_part], axis=-1)
    reach = (SEG_MOST - 1) // token_count + 1
    earlier_pieces = []
    for distance in range(1, reach + 1):
        earlier_pieces.append(passed_along_2(key_value, "ep", distance))
    window = jnp.concatenate(earlier_pieces[::-1] + [key_value], axis=0)
    key_index = (
        first_index - reach * token_count + jnp.arange((reach + 1) * token_count, dtype=jnp.int32)
    )
    query_rows = query.reshape(token_count * head_count, head_dim)
    query_index = jnp.repeat(global_index, head_count)
    query_start = jnp.repeat(start_index, head_count)
    score_scale = 1.0 / math.sqrt(head_dim)
    scores = (
        jnp.einsum(
            "qd,kd->qk", query_rows, window[:, :head_dim], preferred_element_type=jnp.float32
        )
        * score_scale
    )
    allowed = (key_index[None, :] <= query_index[:, None]) & (
        key_index[None, :] >= query_start[:, None]
    )
    probabilities = jnp.where(allowed, jnp.exp(scores), 0.0)
    total_mass = jnp.sum(probabilities, axis=-1)
    mixed = jnp.dot(
        probabilities.astype(jnp.bfloat16), window[:, head_dim:], preferred_element_type=jnp.float32
    )
    attended = (mixed / total_mass[:, None]).astype(jnp.bfloat16).reshape(token_count, query_width)
    return (layer_out[None], attended[None])


def solution(mesh):
    in_specs = (
        P("section", "ep", None),
        P("section", "ep", None),
        P("section", "ep", None),
        P("section", "ep", None, None),
        P("section", "ep", None, None),
        P("section", "ep", None, None),
        P("section", "ep", None),
        P("section", "ep", None),
        P("section", None),
        P("section", None),
        P("section", "ep"),
    )
    out_specs = (P("section", "ep", None), P("section", "ep", None))
    return jax.shard_map(
        on_device, mesh=mesh, in_specs=in_specs, out_specs=out_specs, check_vma=False
    )
```

profile of v0, /device:TPU:7, one launch (start us, length us, event | category | flops | bytes accessed | tf_op | source)
XLA Modules:
  0.0 426.1 jit_solution(1469618486992982408)
XLA Ops:
  7.2 0.9 fusion.58
  8.8 1.5 fusion.10
  10.8 1.7 convolution_convert_fusion.1
  12.6 2.5 broadcast_in_dim.94
  15.1 5.8 %all-to-all-start = ((bf16[8,64,4096]{2,1,0:T(8,128)(2,1)}), bf16[8,64,4096]{2,1,0:T(8,128)(2,1)}, u32[]{:S(2)}, u32[]{:S(2)}) async-start(bf16[8,64,4096]{2,1,0:T(8,128)(2,1)} %bitcast.122), calls=%async_computation | async-start | bytes 8388608 | tf_op jit(solution)/shard_map/all_to_all | solution.py:114
  22.3 116.3 %all-to-all-done = bf16[8,64,4096]{2,1,0:T(8,128)(2,1)} async-done(((bf16[8,64,4096]{2,1,0:T(8,128)(2,1)}), bf16[8,64,4096]{2,1,0:T(8,128)(2,1)}, u32[]{:S(2)}, u32[]{:S(2)}) %all-to-all-start) | async-done | bytes 4194336 | tf_op jit(solution)/shard_map/all_to_all | solution.py:114
  138.6 5.6 %fusion.5 = f32[512,384]{1,0:T(8,128)S(1)} fusion(bf16[512,4096]{1,0:T(8,128)(2,1)} %bitcast.8, bf16[1,1,4096,384]{3,2,1,0:T(8,128)(2,1)} %param.16), kind=kOutput, calls=%fused_computation.11 | convolution fusion | flops 1610612736 | bytes 8126464 | tf_op jit(solution)/shard_map/dot_general | solution.py:61
  144.2 4.6 %fusion.25 = bf16[512,384]{1,0:T(8,128)(2,1)S(1)} fusion(bf16[512,4096]{1,0:T(8,128)(2,1)} %bitcast.8, bf16[1,1,4096,384]{3,2,1,0:T(8,128)(2,1)S(1)} %copy-done.6, f32[512,384]{1,0:T(8,128)S(1)} %fusion.5), kind=kOutput, calls=%fused_computation.35 | convolution fusion | flops 1611792384 | bytes 8519680 | tf_op jit(solution)/shard_map/dot_general | solution.py:62
  148.8 4.3 %convolution_convert_fusion = bf16[8,64,4096]{2,1,0:T(8,128)(2,1)} fusion(bf16[8,64,384]{2,1,0:T(8,128)(2,1)S(1)} %bitcast.132, bf16[1,1,384,4096]{3,2,1,0:T(8,128)(2,1)S(1)} %copy-done), kind=kOutput, calls=%fused_computation.6 | convolution fusion | flops 1612709888 | bytes 7733248 | tf_op jit(solution)/shard_map/dot_general | solution.py:64
  153.1 4.8 %all-to-all-start.1 = ((bf16[8,64,4096]{2,1,0:T(8,128)(2,1)}), bf16[8,64,4096]{2,1,0:T(8,128)(2,1)}, u32[]{:S(2)}, u32[]{:S(2)}) async-start(bf16[8,64,4096]{2,1,0:T(8,128)(2,1)} %convolution_convert_fusion), calls=%async_computation.1 | async-start | bytes 8388608 | tf_op jit(solution)/shard_map/all_to_all | solution.py:118
  160.1 1.2 bitcast_dynamic-update-slice_fusion.1
  161.4 1.2 bitcast_dynamic-update-slice_fusion
  162.6 165.9 %all-reduce.2 = (s32[8]{0:T(128)S(1)}, s32[8]{0:T(128)S(1)}) all-reduce(s32[8]{0:T(128)S(1)} %bitcast_dynamic-update-slice_fusion.1, s32[8]{0:T(128)S(1)} %bitcast_dynamic-update-slice_fusion), channel_id=1, replica_groups=mesh['section'=4,'ep'=8] {'ep'}, use_global_device_ids=true, to_apply=%add | all-reduce | flops 16 | bytes 128
  328.6 30.0 %while.15 = (s32[]{:T(128)}, s32[1]{0:T(128)}, s32[1]{0:T(128)}, s32[]{:T(128)}, s32[8,1]{0,1:T(1,128)S(1)}, /*index=5*/s32[8,1]{0,1:T(1,128)S(1)}, s32[]{:T(128)}) while((s32[]{:T(128)}, s32[1]{0:T(128)}, s32[1]{0:T(128)}, s32[]{:T(128)}, s32[8,1]{0,1:T(1,128)S(1)}, /*index=5*/s32[8,1]{0,1:T(1,128)S(1)}, s32[]{:T(128)}) %tuple.53), condition=%wide.region_9.10_spmd, body=%wide.region_8.9_spmd.sunk | while | flops 11 | bytes 216 | solution.py:37
  359.0 4.5 %convert_reduce_fusion = f32[2,64,4096]{2,1,0:T(8,128)} fusion(bf16[8,64,4096]{2,1,0:T(8,128)(2,1)} %all-to-all-done.1), kind=kLoop, calls=%fused_computation.3 | loop fusion | flops 3670016 | bytes 6291456 | tf_op jit(solution)/shard_map/reduce_sum | solution.py:121
  363.6 5.1 %gather_fusion = f32[128,4096]{1,0:T(8,128)} fusion(f32[128,4096]{1,0:T(8,128)} %bitcast.121, s32[1024]{0:T(1024)S(1)} %pad_clamp_fusion), kind=kCustom, calls=%fused_computation | custom fusion | bytes 4194816 | tf_op jit(solution)/shard_map/jit(_take)/gather | solution.py:124
  368.7 3.4 fusion.12
  372.1 1.4 collective-permute-start
  373.8 3.4 fusion.13
  377.3 8.3 %collective-permute-done = bf16[128,4096]{1,0:T(8,128)(2,1)} collective-permute-done((bf16[128,4096]{1,0:T(8,128)(2,1)}, bf16[128,4096]{1,0:T(8,128)(2,1)}, u32[]{:S(2)}, u32[]{:S(2)}) %collective-permute-start) | collective-permute-done | bytes 1048608 | tf_op jit(solution)/shard_map/ppermute | solution.py:20
  385.5 1.5 fusion.14
  387.1 2.4 fusion.16
  390.0 1.9 collective-permute-start.1
  391.9 1.9 collective-permute-start.2
  393.8 6.9 %collective-permute-start.3 = (bf16[128,256]{1,0:T(8,128)(2,1)S(1)}, bf16[128,256]{1,0:T(8,128)(2,1)}, u32[]{:S(2)}, u32[]{:S(2)}) collective-permute-start(bf16[128,256]{1,0:T(8,128)(2,1)S(1)} %pad_maximum_fusion.2), channel_id=1, source_target_pairs={{0,2},{1,3},{2,4},{3,5},{4,6},{5,7},{8,10},{9,11},{10,12},{11,13},... | collective-permute-start | bytes 196616 | tf_op jit(solution)/shard_map/ppermute | solution.py:43
  400.7 1.9 collective-permute-start.4
  402.6 5.0 %fusion = f32[128,1024]{1,0:T(8,128)S(1)} fusion(bf16[1,4096,1024]{2,1,0:T(8,128)(2,1)} %all-gather.5.cloned.1.call-done, bf16[128,4096]{1,0:T(8,128)(2,1)} %collective-permute-done, f32[128]{0:T(128)S(1)} %add_rsqrt_fusion.2), kind=kOutput, calls=%fused_computation.4 | convolution fusion | flops 1075314688 | bytes 9961984 | tf_op jit(solution)/shard_map/dot_general | solution.py:132
  408.8 0.9 multiply_multiply_fusion
  409.7 1.1 fusion.36
  410.8 1.9 reshape.297
  412.8 0.8 constant_dynamic-update-slice_fusion.4
  415.4 2.5 fusion.59
  (80 shorter events, 15.3 us)
Async XLA Ops:
  7.2 141.6 %copy-start = (bf16[1,1,384,4096]{3,2,1,0:T(8,128)(2,1)S(1)}, bf16[1,1,384,4096]{3,2,1,0:T(8,128)(2,1)}, u32[]{:S(2)}) copy-start(bf16[1,1,384,4096]{3,2,1,0:T(8,128)(2,1)} %param.18) | copy-start | bytes 9437188
  15.1 123.5 %all-to-all-start = ((bf16[8,64,4096]{2,1,0:T(8,128)(2,1)}), bf16[8,64,4096]{2,1,0:T(8,128)(2,1)}, u32[]{:S(2)}, u32[]{:S(2)}) async-start(bf16[8,64,4096]{2,1,0:T(8,128)(2,1)} %bitcast.122), calls=%async_computation | async-start | bytes 8388608 | tf_op jit(solution)/shard_map/all_to_all | solution.py:114
  20.8 366.3 %all-gather.7.cloned.1.call-start = ((), (), s32[]{:S(2)}) async-start(), calls=%async_computation.3 | async-start | bytes 2359296 | tf_op jit(solution)/shard_map/all_gather | solution.py:139
  21.5 381.1 %all-gather.5.cloned.1.call-start = ((), (), s32[]{:S(2)}) async-start(), calls=%async_computation.2 | async-start | bytes 9437184 | tf_op jit(solution)/shard_map/all_gather | solution.py:134
  138.6 5.6 %copy-start.6 = (bf16[1,1,4096,384]{3,2,1,0:T(8,128)(2,1)S(1)}, bf16[1,1,4096,384]{3,2,1,0:T(8,128)(2,1)}, u32[]{:S(2)}) copy-start(bf16[1,1,4096,384]{3,2,1,0:T(8,128)(2,1)} %param.17) | copy-start | bytes 9437188
  153.1 4.8 %copy-start.5 = (s32[1,128]{1,0:T(1,128)S(1)}, s32[1,128]{1,0:T(1,128)}, u32[]{:S(2)}) copy-start(s32[1,128]{1,0:T(1,128)} %param.23) | copy-start | bytes 1540
  153.1 6.4 %copy-start.7 = (u32[32]{0:T(128)S(1)}, u32[32]{0:T(128)}, u32[]{:S(2)}) copy-start(u32[32]{0:T(128)} %constant.111) | copy-start | bytes 388
  153.1 205.5 %copy-start.2 = (s32[1,128,8]{1,2,0:T(8,128)S(1)}, s32[1,128,8]{1,2,0:T(8,128)}, u32[]{:S(2)}) copy-start(s32[1,128,8]{1,2,0:T(8,128)} %param.14) | copy-start | bytes 12292
  153.1 205.6 %copy-start.3 = (f32[1,128,8]{1,2,0:T(8,128)S(1)}, f32[1,128,8]{1,2,0:T(8,128)}, u32[]{:S(2)}) copy-start(f32[1,128,8]{1,2,0:T(8,128)} %param.15) | copy-start | bytes 12292
  153.1 205.9 %all-to-all-start.1 = ((bf16[8,64,4096]{2,1,0:T(8,128)(2,1)}), bf16[8,64,4096]{2,1,0:T(8,128)(2,1)}, u32[]{:S(2)}, u32[]{:S(2)}) async-start(bf16[8,64,4096]{2,1,0:T(8,128)(2,1)} %convolution_convert_fusion), calls=%async_computation.1 | async-start | bytes 8388608 | tf_op jit(solution)/shard_map/all_to_all | solution.py:118
  372.1 13.5 %collective-permute-start = (bf16[128,4096]{1,0:T(8,128)(2,1)}, bf16[128,4096]{1,0:T(8,128)(2,1)}, u32[]{:S(2)}, u32[]{:S(2)}) collective-permute-start(bf16[128,4096]{1,0:T(8,128)(2,1)} %fusion.12), channel_id=1, source_target_pairs={{24,0},{0,8},{8,16},{16,24},{25,1},{1,9},{9,17},{17,25},{26,2},{2,... | collective-permute-start | bytes 3145736 | tf_op jit(solution)/shard_map/ppermute | solution.py:20
  377.3 12.4 %copy-start.4 = (f32[1,128]{1,0:T(1,128)S(1)}, f32[1,128]{1,0:T(1,128)}, u32[]{:S(2)}) copy-start(f32[1,128]{1,0:T(1,128)} %param.22) | copy-start | bytes 1540
  390.0 22.8 %collective-permute-start.1 = (bf16[128,256]{1,0:T(8,128)(2,1)S(1)}, bf16[128,256]{1,0:T(8,128)(2,1)}, u32[]{:S(2)}, u32[]{:S(2)}) collective-permute-start(bf16[128,256]{1,0:T(8,128)(2,1)S(1)} %pad_maximum_fusion.2), channel_id=1, source_target_pairs={{0,4},{1,5},{2,6},{3,7},{8,12},{9,13},{10,14},{11,15},{16,20},{17,... | collective-permute-start | bytes 196616 | tf_op jit(solution)/shard_map/ppermute | solution.py:43
  391.9 21.8 %collective-permute-start.2 = (bf16[128,256]{1,0:T(8,128)(2,1)S(1)}, bf16[128,256]{1,0:T(8,128)(2,1)}, u32[]{:S(2)}, u32[]{:S(2)}) collective-permute-start(bf16[128,256]{1,0:T(8,128)(2,1)S(1)} %pad_maximum_fusion.2), channel_id=1, source_target_pairs={{0,3},{1,4},{2,5},{3,6},{4,7},{8,11},{9,12},{10,13},{11,14},{12,15... | collective-permute-start | bytes 196616 | tf_op jit(solution)/shard_map/ppermute | solution.py:43
  393.8 20.7 %collective-permute-start.3 = (bf16[128,256]{1,0:T(8,128)(2,1)S(1)}, bf16[128,256]{1,0:T(8,128)(2,1)}, u32[]{:S(2)}, u32[]{:S(2)}) collective-permute-start(bf16[128,256]{1,0:T(8,128)(2,1)S(1)} %pad_maximum_fusion.2), channel_id=1, source_target_pairs={{0,2},{1,3},{2,4},{3,5},{4,6},{5,7},{8,10},{9,11},{10,12},{11,13},... | collective-permute-start | bytes 196616 | tf_op jit(solution)/shard_map/ppermute | solution.py:43
  400.7 14.7 %collective-permute-start.4 = (bf16[128,256]{1,0:T(8,128)(2,1)S(1)}, bf16[128,256]{1,0:T(8,128)(2,1)S(1)}, u32[]{:S(2)}, u32[]{:S(2)}) collective-permute-start(bf16[128,256]{1,0:T(8,128)(2,1)S(1)} %pad_maximum_fusion.2), channel_id=1, source_target_pairs={{0,1},{1,2},{2,3},{3,4},{4,5},{5,6},{6,7},{8,9},{9,10},{10,11},{11... | collective-permute-start | bytes 196616 | tf_op jit(solution)/shard_map/ppermute | solution.py:43
  407.6 0.8 copy-start.1
Sparse Core Ops, SparseCore 0:
  23.8 103.2 all-gather.6
  129.2 203.0 all-gather.4
where the time goes:
time: 433 us; the launch traced here: 426 us
  blocking collectives  166 us (38%)
  waiting for transfers between devices  126 us (29%)
  matrix products  26.7 us (6%)
  loops' own time  25.2 us (6%)
  starting transfers between devices  24.6 us (6%)
  local copies, waits for them, and re-layouts  23.3 us (5%)
  other arithmetic  20 us (5%)
  between operations  14.4 us (3%)
    unnamed x1, blocking collectives  166 us
    all_to_all x1, waiting for transfers between devices, on_device(): lax.all_to_all(spread, 'ep', split_axis=0, concat_axis=0, tiled=True)  116 us
    another operation x1, loops' own time, prefix(): return lax.fori_loop(0, length, step, start)  25.2 us
    ppermute x4, starting transfers between devices, passed_along_2(): lax.ppermute(value, axis, [(source, source + steps) for source in range(l...  12.6 us
  transfers between devices with their start and end apart: 9, of which 2 were waited for; matrix products, arithmetic and copies ran while one was open for 13% of the time, Pallas kernels for 0%

commit v1 on v0

--- a/solution.py
+++ b/solution.py
@@ -3,6 +3,8 @@
 import jax
 import jax.numpy as jnp
 from jax import lax
+from jax.experimental import pallas as pl
+from jax.experimental.pallas import tpu as pltpu
 from jax.sharding import PartitionSpec as P
 
 OWNERS = 4
@@ -190,6 +192,387 @@
     return (layer_out[None], attended[None])
 
 
+MESH = pl.DeviceIdType.MESH
+CHUNKS = 4
+
+
+def fused_kernel(
+    tok_ref, route_ref, rw_ref, wg_hbm, wu_hbm, wd_hbm, wq_hbm, wkv_hbm,
+    gq_ref, gk_ref, segrow_ref, segcol_ref, freq_ref,
+    lo_ref, att_ref,
+    xbuf, other, wgu, wd, act, pd, py, pz, own, r1, r2y, r2z, sm, rm,
+    lo, lbuf, wbuf, rbuf, scale_out, scale_in, kv, segs, place_s,
+    load_sem, send_sem, recv_sem, l_send, l_recv, p_send, p_recv,
+    kv_send, kv_recv, seg_send, seg_recv,
+):
+    f32, bf16 = jnp.float32, jnp.bfloat16
+    section = lax.axis_index("section")
+    sections = lax.axis_size("section")
+    me = lax.axis_index("ep")
+    count = lax.axis_size("ep")
+    z, y = me // 2, me % 2
+    expert = z // 2
+    token_count, width = tok_ref.shape
+    half = token_count // 2
+    piece = width // CHUNKS
+    y_peer = z * 2 + (1 - y)
+    z_peer = (z // 2 * 2 + 1 - z % 2) * 2 + y
+    mirror = lax.rem(z + 2, 4) * 2 + y
+    following = lax.rem(section + 1, sections)
+    preceding = lax.rem(section + sections - 1, sections)
+
+    barrier = pltpu.get_barrier_semaphore()
+    for k in range(1, 8):
+        pl.semaphore_signal(
+            barrier, inc=1, device_id=(section, lax.rem(me + k, count)), device_id_type=MESH
+        )
+    for k in range(4):
+        pl.semaphore_signal(barrier, inc=1, device_id=(preceding, k * 2 + y), device_id_type=MESH)
+
+    hidden_parts = wgu.shape[0]
+    loads = []
+    for j in range(hidden_parts):
+        cols = pl.ds(j * 128, 128)
+        loads.append((wg_hbm.at[:, cols], wgu.at[j, :, pl.ds(0, 128)]))
+        loads.append((wu_hbm.at[:, cols], wgu.at[j, :, pl.ds(128, 128)]))
+    loads.append((wd_hbm, wd))
+    query_width = wq_hbm.shape[1]
+    loads.append((wq_hbm, wbuf.at[y, :, pl.ds(0, query_width)]))
+    loads.append((wkv_hbm, wbuf.at[y, :, pl.ds(query_width, wkv_hbm.shape[1])]))
+    loads = [
+        pltpu.make_async_copy(src, dst, load_sem.at[i]) for i, (src, dst) in enumerate(loads)
+    ]
+    for load in loads:
+        load.start()
+
+    def remote(src, dst, i, target):
+        return pltpu.make_async_remote_copy(
+            src_ref=src, dst_ref=dst, send_sem=send_sem.at[i], recv_sem=recv_sem.at[i],
+            device_id=(section, target), device_id_type=MESH,
+        )
+
+    low, high = pl.ds(0, half), pl.ds(half, half)
+    c0 = remote(other, xbuf.at[0, high], 0, mirror)
+    c1 = remote(xbuf.at[0, low], xbuf.at[1, low], 1, y_peer)
+    c2 = remote(xbuf.at[0, low], xbuf.at[2, low], 2, z_peer)
+    c3 = remote(xbuf.at[0, high], xbuf.at[1, high], 3, y_peer)
+    c4 = remote(xbuf.at[0, high], xbuf.at[2, high], 4, z_peer)
+    c5 = remote(xbuf.at[1, low], xbuf.at[3, low], 5, z_peer)
+    c6 = remote(xbuf.at[2, high], xbuf.at[3, high], 6, y_peer)
+    first_hop = []
+    for c in range(CHUNKS):
+        first_hop.append(remote(pd.at[c], r1.at[c], 7 + c, z_peer if c < 2 else y_peer))
+    to_y = [remote(py.at[c], r2y.at[c], 11 + c, y_peer) for c in range(CHUNKS)]
+    to_z = [remote(pz.at[c], r2z.at[c], 15 + c, z_peer) for c in range(CHUNKS)]
+    to_mirror = [remote(sm.at[c], rm.at[c], 19 + c, mirror) for c in range(CHUNKS)]
+    weights = remote(wbuf.at[y], wbuf.at[y], 23, y_peer)
+    weights_in = remote(wbuf.at[1 - y], wbuf.at[1 - y], 23, y_peer)
+
+    squares = jnp.zeros((token_count, 1), f32)
+    for c in range(CHUNKS):
+        part = tok_ref[:, c * piece : (c + 1) * piece].astype(f32)
+        squares += jnp.sum(part * part, axis=-1, keepdims=True)
+    inverse = lax.rsqrt(squares / width + EPSILON)
+    routes = route_ref[...]
+    inside = routes < 2
+    has_route = jnp.sum(jnp.where(inside, 1.0, 0.0), axis=-1, keepdims=True)
+    chosen = jnp.sum(jnp.where(inside, routes.astype(f32), 0.0), axis=-1, keepdims=True)
+    weight = jnp.sum(jnp.where(inside, rw_ref[...], 0.0), axis=-1, keepdims=True)
+    group = jnp.where(chosen == expert.astype(f32), 0.0, 1.0)
+    lane_i = lax.broadcasted_iota(jnp.int32, (token_count, token_count), 1)
+    row_i = lax.broadcasted_iota(jnp.int32, (token_count, token_count), 0)
+    lane = lane_i.astype(f32)
+    groups = jnp.where(lane == group, has_route, 0.0)
+    before = jnp.where(lane_i < row_i, 1.0, 0.0)
+    ranks = jnp.dot(before.astype(bf16), groups.astype(bf16), preferred_element_type=f32)
+    rank = jnp.sum(ranks * groups, axis=-1, keepdims=True)
+    placing = jnp.where(lane == group * half + rank, has_route, 0.0).astype(bf16)
+    place_s[...] = placing
+    for c in range(CHUNKS):
+        cols = slice(c * piece, (c + 1) * piece)
+        normed = (tok_ref[:, cols].astype(f32) * inverse).astype(bf16)
+        packed = lax.dot_general(
+            placing, normed, (((0,), (0,)), ((), ())), preferred_element_type=f32
+        ).astype(bf16)
+        xbuf[0, 0:half, cols] = packed[:half]
+        other[:, cols] = packed[half:]
+
+    pl.semaphore_wait(barrier, 11)
+    c0.start()
+    c1.start()
+    c2.start()
+    seg_copies = []
+    for k in range(1, 8):
+        copy = pltpu.make_async_remote_copy(
+            src_ref=segrow_ref, dst_ref=segs.at[k - 1],
+            send_sem=seg_send.at[k - 1], recv_sem=seg_recv.at[k - 1],
+            device_id=(section, lax.rem(me + k, count)), device_id_type=MESH,
+        )
+        copy.start()
+        seg_copies.append(copy)
+
+    def expert_rows(q):
+        def step(j, carry):
+            both = jnp.dot(xbuf[q], wgu[j], preferred_element_type=f32)
+            gate, up = both[:, :128], both[:, 128:]
+            act[j] = (gate / (1.0 + jnp.exp(-gate)) * up).astype(bf16)
+            return carry
+
+        lax.fori_loop(0, hidden_parts, step, 0)
+        return jnp.concatenate([act[j] for j in range(hidden_parts)], axis=-1)
+
+    def down(rows, c):
+        return jnp.dot(
+            rows, wd[:, c * piece : (c + 1) * piece], preferred_element_type=f32
+        )
+
+    c1.wait_recv()
+    c5.start()
+    c0.wait_recv()
+    c3.start()
+    c4.start()
+    for load in loads:
+        load.wait()
+    rows = expert_rows(0)
+    for c in range(CHUNKS):
+        own[c] = down(rows, c)
+    c2.wait_recv()
+    c4.wait_recv()
+    c6.start()
+    rows = expert_rows(2)
+    for c in range(CHUNKS):
+        pz[c] = down(rows, c).astype(bf16)
+        if c < 2:
+            to_z[c].start()
+    c3.wait_recv()
+    rows = expert_rows(1)
+    for c in (2, 3, 0, 1):
+        py[c] = down(rows, c).astype(bf16)
+        if c >= 2:
+            to_y[c].start()
+    c5.wait_recv()
+    c6.wait_recv()
+    rows = expert_rows(3)
+    for c in (0, 2, 1, 3):
+        pd[c] = down(rows, c).astype(bf16)
+        first_hop[c].start()
+    for c in (0, 2, 1, 3):
+        first_hop[c].wait_recv()
+        if c < 2:
+            py[c] = (py[c].astype(f32) + r1[c].astype(f32)).astype(bf16)
+            to_y[c].start()
+        else:
+            pz[c] = (pz[c].astype(f32) + r1[c].astype(f32)).astype(bf16)
+            to_z[c].start()
+    weights.start()
+    order = (0, 2, 1, 3)
+    for c in order:
+        to_y[c].wait_recv()
+        to_z[c].wait_recv()
+        total = own[c] + r2y[c].astype(f32) + r2z[c].astype(f32)
+        own[c] = total
+        sm[c] = total[half:].astype(bf16)
+        to_mirror[c].start()
+
+    def onward(c):
+        return pltpu.make_async_remote_copy(
+            src_ref=lo.at[c], dst_ref=lbuf.at[z], send_sem=l_send.at[c], recv_sem=l_recv.at[z],
+            device_id=(following, c * 2 + y), device_id_type=MESH,
+        )
+
+    squares = jnp.zeros((token_count, 1), f32)
+    for c in order:
+        to_mirror[c].wait_recv()
+        merged = jnp.concatenate([own[c][:half].astype(bf16), rm[c]], axis=0)
+        spread = jnp.dot(place_s[...], merged, preferred_element_type=f32)
+        cols = slice(c * piece, (c + 1) * piece)
+        result = (tok_ref[:, cols].astype(f32) + weight * spread).astype(bf16)
+        lo[c] = result
+        onward(c).start()
+        lo_ref[:, cols] = result
+        wide = result.astype(f32)
+        squares += jnp.sum(wide * wide, axis=-1, keepdims=True)
+    scale_out[...] = jnp.broadcast_to(
+        lax.rsqrt(squares / width + EPSILON), scale_out.shape
+    )
+    scale_copy = pltpu.make_async_remote_copy(
+        src_ref=scale_out, dst_ref=scale_in, send_sem=send_sem.at[24], recv_sem=recv_sem.at[24],
+        device_id=(following, me), device_id_type=MESH,
+    )
+    scale_copy.start()
+
+    for copy in seg_copies:
+        copy.wait_recv()
+    mine = segcol_ref[...]
+    start = jnp.sum(
+        jnp.where(segrow_ref[...] < mine, 1.0, 0.0), axis=-1, keepdims=True
+    )
+    for k in range(7):
+        start += jnp.sum(jnp.where(segs[k] < mine, 1.0, 0.0), axis=-1, keepdims=True)
+    index = (
+        lax.broadcasted_iota(jnp.int32, (token_count, 1), 0) + me * token_count
+    ).astype(f32)
+    angles = (index - start) * freq_ref[...]
+    head_dim = gq_ref.shape[-1]
+    cosine = jnp.cos(angles)
+    lanes = lax.broadcasted_iota(jnp.int32, (token_count, head_dim), 1)
+    sine = jnp.where(lanes < head_dim // 2, -1.0, 1.0) * jnp.sin(angles)
+
+    weights_in.wait_recv()
+
+    def project(rows):
+        result = jnp.dot(rows[:, : piece // 2], wbuf[0], preferred_element_type=f32)
+        result += jnp.dot(rows[:, piece // 2 :], wbuf[1], preferred_element_type=f32)
+        return result.astype(bf16)
+
+    def arrival(source):
+        return pltpu.make_async_remote_copy(
+            src_ref=lo.at[0], dst_ref=lbuf.at[source], send_sem=l_send.at[0],
+            recv_sem=l_recv.at[source], device_id=(preceding, source * 2 + y),
+            device_id_type=MESH,
+        )
+
+    def partial_copy(k):
+        target = lax.rem(z + k, 4)
+        return pltpu.make_async_remote_copy(
+            src_ref=lbuf_out(k), dst_ref=rbuf.at[k - 1], send_sem=p_send.at[k - 1],
+            recv_sem=p_recv.at[k - 1], device_id=(section, target * 2 + y), device_id_type=MESH,
+        )
+
+    def lbuf_out(k):
+        return rbuf.at[2 + k]
+
+    for k in (2, 1, 3):
+        source = lax.rem(z + k, 4)
+        arrival(source).wait_recv()
+        rbuf[2 + k] = project(lbuf[source])
+        partial_copy(k).start()
+    arrival(z).wait_recv()
+    mixed = project(lbuf[z]).astype(f32)
+    scale_copy.wait_recv()
+    for k in range(1, 4):
+        partial_copy(k).wait_recv()
+        mixed += rbuf[k - 1].astype(f32)
+    mixed *= scale_in[:, 0:1]
+
+    def turn(values, gain):
+        values = values * lax.rsqrt(jnp.mean(values * values, axis=-1, keepdims=True) + EPSILON)
+        values = values * gain
+        return values * cosine + pltpu.roll(values, head_dim // 2, 1) * sine
+
+    key = turn(mixed[:, query_width : query_width + head_dim], gk_ref[...]).astype(bf16)
+    kv[0, :, 0:head_dim] = key
+    kv[0, :, head_dim:] = mixed[:, query_width + head_dim :].astype(bf16)
+    reach = kv.shape[0] - 1
+    kv_copies = []
+    for k in range(1, reach + 1):
+        copy = pltpu.make_async_remote_copy(
+            src_ref=kv.at[0], dst_ref=kv.at[k], send_sem=kv_send.at[k - 1],
+            recv_sem=kv_recv.at[k - 1], device_id=(section, lax.rem(me + k, count)),
+            device_id_type=MESH,
+        )
+        copy.start()
+        kv_copies.append(copy)
+    queries = [
+        turn(mixed[:, h * head_dim : (h + 1) * head_dim], gq_ref[...]).astype(bf16)
+        for h in range(query_width // head_dim)
+    ]
+    for copy in kv_copies:
+        copy.wait_recv()
+    key_count = (reach + 1) * token_count
+    place = lax.broadcasted_iota(jnp.int32, (1, key_count), 1)
+    slot = place // token_count
+    key_index = (lax.rem(me - slot + count, count) * token_count + place % token_count).astype(f32)
+    allowed = (key_index <= index) & (key_index >= start)
+    everything = kv[...].reshape(key_count, 2 * head_dim)
+    keys, values = everything[:, :head_dim], everything[:, head_dim:]
+    for h, query in enumerate(queries):
+        scores = lax.dot_general(
+            query, keys, (((1,), (1,)), ((), ())), preferred_element_type=f32
+        ) * (1.0 / math.sqrt(head_dim))
+        probs = jnp.where(allowed, jnp.exp(scores), 0.0)
+        mass = jnp.sum(probs, axis=-1, keepdims=True)
+        out = jnp.dot(probs.astype(bf16), values, preferred_element_type=f32) / mass
+        att_ref[:, h * head_dim : (h + 1) * head_dim] = out.astype(bf16)
+
+    for copy in [c0, c1, c2, c3, c4, c5, c6, weights, scale_copy]:
+        copy.wait_send()
+    for copy in first_hop + to_y + to_z + to_mirror + seg_copies + kv_copies:
+        copy.wait_send()
+    for c in range(CHUNKS):
+        onward(c).wait_send()
+    for k in range(1, 4):
+        partial_copy(k).wait_send()
+
+
+def fused_on_device(
+    tokens, routes, router_weights, w_gate, w_up, w_down, w_query, w_keyval,
+    gain_query, gain_key, segment_ids,
+):
+    token_count, width = tokens.shape[1:]
+    half = token_count // 2
+    piece = width // CHUNKS
+    hidden = w_gate.shape[-1]
+    head_dim = gain_query.shape[-1]
+    out_width = w_query.shape[-1] + w_keyval.shape[-1]
+    reach = (SEG_MOST - 1) // token_count + 1
+    half_count = head_dim // 2
+    frequency = ROPE_BASE ** (-(jnp.arange(half_count, dtype=jnp.float32) * 2.0) / head_dim)
+    frequency = jnp.concatenate([frequency, frequency])[None]
+    bf16, f32 = jnp.bfloat16, jnp.float32
+    vmem, hbm = pl.BlockSpec(memory_space=pltpu.VMEM), pl.BlockSpec(memory_space=pl.ANY)
+    chunked = (CHUNKS, token_count, piece)
+    dma = pltpu.SemaphoreType.DMA
+    layer_out, attended = pl.pallas_call(
+        fused_kernel,
+        out_shape=(
+            jax.ShapeDtypeStruct((token_count, width), bf16),
+            jax.ShapeDtypeStruct((token_count, w_query.shape[-1]), bf16),
+        ),
+        in_specs=[vmem] * 3 + [hbm] * 5 + [vmem] * 5,
+        out_specs=(vmem, vmem),
+        scratch_shapes=[
+            pltpu.VMEM((4, token_count, width), bf16),
+            pltpu.VMEM((half, width), bf16),
+            pltpu.VMEM((hidden // 128, width, 256), bf16),
+            pltpu.VMEM((hidden, width), bf16),
+            pltpu.VMEM((hidden // 128, token_count, 128), bf16),
+            pltpu.VMEM(chunked, bf16),
+            pltpu.VMEM(chunked, bf16),
+            pltpu.VMEM(chunked, bf16),
+            pltpu.VMEM(chunked, f32),
+            pltpu.VMEM(chunked, bf16),
+            pltpu.VMEM(chunked, bf16),
+            pltpu.VMEM(chunked, bf16),
+            pltpu.VMEM((CHUNKS, half, piece), bf16),
+            pltpu.VMEM((CHUNKS, half, piece), bf16),
+            pltpu.VMEM(chunked, bf16),
+            pltpu.VMEM(chunked, bf16),
+            pltpu.VMEM((2, w_query.shape[1], out_width), bf16),
+            pltpu.VMEM((6, token_count, out_width), bf16),
+            pltpu.VMEM((token_count, 128), f32),
+            pltpu.VMEM((token_count, 128), f32),
+            pltpu.VMEM((reach + 1, token_count, 2 * head_dim), bf16),
+            pltpu.VMEM((7, 1, token_count), jnp.int32),
+            pltpu.VMEM((token_count, token_count), bf16),
+            dma((16,)),
+            dma((25,)), dma((25,)),
+            dma((4,)), dma((4,)),
+            dma((3,)), dma((3,)),
+            dma((reach,)), dma((reach,)),
+            dma((7,)), dma((7,)),
+        ],
+        compiler_params=pltpu.CompilerParams(
+            collective_id=0, has_side_effects=True, vmem_limit_bytes=56 * 1024 * 1024
+        ),
+    )(
+        tokens[0], routes[0], router_weights[0], w_gate[0, 0], w_up[0, 0], w_down[0, 0],
+        w_query[0], w_keyval[0], gain_query, gain_key, segment_ids,
+        segment_ids.reshape(token_count, 1), frequency,
+    )
+    return (layer_out[None], attended[None])
+
+
 def solution(mesh):
     in_specs = (
         P("section", "ep", None),
@@ -206,5 +589,5 @@
     )
     out_specs = (P("section", "ep", None), P("section", "ep", None))
     return jax.shard_map(
-        on_device, mesh=mesh, in_specs=in_specs, out_specs=out_specs, check_vma=False
-    )
+        fused_on_device if mesh.shape["ep"] == 8 else on_device, mesh=mesh, in_specs=in_specs, out_specs=out_specs, check_vma=False
+    )

time: 433 us -> 192 us (0.44); the launches traced: 426 us -> 192 us
  Pallas kernels: 0 us -> 183 us
  blocking collectives: 166 us -> 0 us
  waiting for transfers between devices: 126 us -> 0 us
  matrix products: 26.7 us -> 0 us
  loops' own time: 25.2 us -> 0 us
  starting transfers between devices: 24.6 us -> 0 us
  other arithmetic: 20 us -> 0.67 us
  local copies, waits for them, and re-layouts: 23.3 us -> 8.17 us
  between operations: 14.4 us -> 0.64 us
    pallas_call x0 -> x1, Pallas kernels: none -> 183 us  [fused_on_device(): pl.pallas_call(fused_kernel, out_shape=(jax.ShapeDtypeStruct((token_count...]
    unnamed x1 -> x0, blocking collectives: 166 us -> none
    all_to_all x2 -> x0, waiting for transfers between devices: 116 us -> none  [the longest x1 116 us: on_device(): lax.all_to_all(spread, 'ep', split_axis=0, concat_axis=0, tiled=True)]
    dot_general x8 -> x0, matrix products: 26.7 us -> none  [the longest x1 5.62 us: feed_forward(): jnp.dot(row_block, gate_part, preferred_element_type=jnp.float32)]
    another operation x1 -> x0, loops' own time: 25.2 us -> none  [prefix(): return lax.fori_loop(0, length, step, start)]
    ppermute x5 -> x0, starting transfers between devices: 14 us -> none  [the longest x4 12.6 us: passed_along_2(): lax.ppermute(value, axis, [(source, source + steps) for source in range(l...]
    all_to_all x2 -> x0, starting transfers between devices: 10.6 us -> none  [the longest x1 5.77 us: on_device(): lax.all_to_all(spread, 'ep', split_axis=0, concat_axis=0, tiled=True)]
    reduce_sum x8 -> x0, other arithmetic: 8.87 us -> none  [the longest x1 4.53 us: on_device(): jnp.sum(returned_rows.reshape(expert_count, OWNERS, capacity, model_width...]
  transfers between devices with their start and end apart: 9 -> 0, of which waited for: 2 -> 0; matrix products, arithmetic and copies ran while one was open for 13% -> 0% of each run, Pallas kernels for 0% -> 0%
where the time goes in v1:
time: 192 us
  Pallas kernels  183 us (95%)
  local copies, waits for them, and re-layouts  8.17 us (4%)
    pallas_call x1, Pallas kernels, fused_on_device(): pl.pallas_call(fused_kernel, out_shape=(jax.ShapeDtypeStruct((token_count...  183 us
    unnamed x4, local copies, waits for them, and re-layouts  6.79 us

profile of v1, /device:TPU:7, one launch (start us, length us, event | category | flops | bytes accessed | tf_op | source)
XLA Modules:
  0.0 192.0 jit_solution(13680631289078146336)
XLA Ops:
  0.6 0.7 maximum_bitcast_fusion.freq_ref
  1.3 1.4 copy.13
  2.7 1.4 copy.14
  4.1 1.4 copy.15.segcol_ref
  5.5 182.5 %shard_map.122 = (bf16[128,4096]{1,0:T(8,128)(2,1)}, bf16[128,1024]{1,0:T(8,128)(2,1)}) custom-call(bf16[128,4096]{1,0:T(8,128)(2,1)} %bitcast.16, s32[128,8]{1,0:T(8,128)} %bitcast.19, f32[128,8]{1,0:T(8,128)} %bitcast.20, bf16[4096,384]{1,0:T(8,128)(2,1)} %bitcast.13, bf16[4096,384]{1,0:T(8,128)(2,1)} %bitcast.14, bf16[384,4096]{1,0:T(8,128)(2,1)} %bitcast.15, ...), custom_call_target="tpu_custom_call" | custom-call | tf_op jit(solution)/shard_map/pallas_call | solution.py:526
  188.0 2.3 %copy.18 = bf16[1,128,4096]{2,1,0:T(8,128)(2,1)} copy(bf16[1,128,4096]{2,1,0:T(8,128)(2,1)} %bitcast.18) | data formatting | bytes 2097152
  190.3 1.7 copy.19
  (1 shorter events, 0.0 us)

commit v2 on v1

--- a/solution.py
+++ b/solution.py
@@ -101,7 +101,10 @@
     weight_kept = jnp.sum(jnp.where(inside, router_weights[0], 0.0), axis=-1)
     expert_ids = jnp.arange(expert_count, dtype=jnp.int32)
     member = ((chosen[:, None] == expert_ids[None, :]) & has_route[:, None]).astype(jnp.int32)
-    rank_within = jnp.sum((jnp.cumsum(member, axis=0) - member) * member, axis=-1)
+    token_ids = jnp.arange(token_count, dtype=jnp.int32)
+    earlier = (token_ids[None, :] < token_ids[:, None]).astype(jnp.float32)
+    ranks = jnp.dot(earlier, member.astype(jnp.float32)).astype(jnp.int32)
+    rank_within = jnp.sum(ranks * member, axis=-1)
     slot_index = jnp.where(has_route, chosen * capacity + rank_within, -1)
     slot_ids = jnp.arange(expert_count * capacity, dtype=jnp.int32)
     placing = (slot_ids[:, None] == slot_index[None, :]).astype(jnp.bfloat16)
@@ -144,8 +147,12 @@
     segment_row = segment_ids[0]
     first_index = lax.axis_index("ep") * token_count
     global_index = first_index + jnp.arange(token_count, dtype=jnp.int32)
-    change = jnp.concatenate([jnp.ones((1,), dtype=bool), segment_row[1:] != segment_row[:-1]])
-    local_start = lax.cummax(jnp.where(change, global_index, 0), axis=0)
+    local_start = jnp.min(
+        jnp.where(
+            segment_row[None, :] == segment_row[:, None], global_index[None, :], FAR_INDEX
+        ),
+        axis=1,
+    )
     empty_prior = (jnp.full((1,), -1, jnp.int32), jnp.full((1,), FAR_INDEX, jnp.int32))
     prior_id, prior_start = prefix(
         (segment_row[-1:], local_start[-1:]), "ep", keep_later, empty_prior
@@ -198,7 +205,7 @@
 
 def fused_kernel(
     tok_ref, route_ref, rw_ref, wg_hbm, wu_hbm, wd_hbm, wq_hbm, wkv_hbm,
-    gq_ref, gk_ref, segrow_ref, segcol_ref, freq_ref,
+    gq_ref, gk_ref, segrow_ref, freq_ref,
     lo_ref, att_ref,
     xbuf, other, wgu, wd, act, pd, py, pz, own, r1, r2y, r2z, sm, rm,
     lo, lbuf, wbuf, rbuf, scale_out, scale_in, kv, segs, place_s,
@@ -252,18 +259,30 @@
         )
 
     low, high = pl.ds(0, half), pl.ds(half, half)
-    c0 = remote(other, xbuf.at[0, high], 0, mirror)
+    blocks = [pl.ds(b * (half // 4), half // 4) for b in range(4)]
+    upper = [pl.ds(half + b * (half // 4), half // 4) for b in range(4)]
+    c0 = [
+        remote(other.at[s], xbuf.at[0, u], 27 + b, mirror)
+        for b, (s, u) in enumerate(zip(blocks, upper))
+    ]
     c1 = remote(xbuf.at[0, low], xbuf.at[1, low], 1, y_peer)
     c2 = remote(xbuf.at[0, low], xbuf.at[2, low], 2, z_peer)
-    c3 = remote(xbuf.at[0, high], xbuf.at[1, high], 3, y_peer)
-    c4 = remote(xbuf.at[0, high], xbuf.at[2, high], 4, z_peer)
+    c3 = [remote(xbuf.at[0, u], xbuf.at[1, u], 31 + b, y_peer) for b, u in enumerate(upper)]
+    c4 = [remote(xbuf.at[0, u], xbuf.at[2, u], 35 + b, z_peer) for b, u in enumerate(upper)]
     c5 = remote(xbuf.at[1, low], xbuf.at[3, low], 5, z_peer)
-    c6 = remote(xbuf.at[2, high], xbuf.at[3, high], 6, y_peer)
-    first_hop = []
-    for c in range(CHUNKS):
-        first_hop.append(remote(pd.at[c], r1.at[c], 7 + c, z_peer if c < 2 else y_peer))
-    to_y = [remote(py.at[c], r2y.at[c], 11 + c, y_peer) for c in range(CHUNKS)]
-    to_z = [remote(pz.at[c], r2z.at[c], 15 + c, z_peer) for c in range(CHUNKS)]
+    c6 = [remote(xbuf.at[2, u], xbuf.at[3, u], 39 + b, y_peer) for b, u in enumerate(upper)]
+    def parts(src, dst, base, target):
+        return {
+            (c, h): remote(
+                src.at[c, pl.ds(h * half, half)], dst.at[c, pl.ds(h * half, half)],
+                base + 2 * c + h, target(c),
+            )
+            for c in range(CHUNKS) for h in range(2)
+        }
+
+    first_hop = parts(pd, r1, 43, lambda c: z_peer if c < 2 else y_peer)
+    to_y = parts(py, r2y, 51, lambda c: y_peer)
+    to_z = parts(pz, r2z, 59, lambda c: z_peer)
     to_mirror = [remote(sm.at[c], rm.at[c], 19 + c, mirror) for c in range(CHUNKS)]
     weights = remote(wbuf.at[y], wbuf.at[y], 23, y_peer)
     weights_in = remote(wbuf.at[1 - y], wbuf.at[1 - y], 23, y_peer)
@@ -273,14 +292,20 @@
         part = tok_ref[:, c * piece : (c + 1) * piece].astype(f32)
         squares += jnp.sum(part * part, axis=-1, keepdims=True)
     inverse = lax.rsqrt(squares / width + EPSILON)
+    lane_i = lax.broadcasted_iota(jnp.int32, (token_count, token_count), 1)
+    row_i = lax.broadcasted_iota(jnp.int32, (token_count, token_count), 0)
+
+    def column(row):
+        return jnp.sum(jnp.where(lane_i == row_i, row, 0.0), axis=-1, keepdims=True)
+
     routes = route_ref[...]
     inside = routes < 2
-    has_route = jnp.sum(jnp.where(inside, 1.0, 0.0), axis=-1, keepdims=True)
-    chosen = jnp.sum(jnp.where(inside, routes.astype(f32), 0.0), axis=-1, keepdims=True)
-    weight = jnp.sum(jnp.where(inside, rw_ref[...], 0.0), axis=-1, keepdims=True)
+    has_route = column(jnp.sum(jnp.where(inside, 1.0, 0.0), axis=0, keepdims=True))
+    chosen = column(
+        jnp.sum(jnp.where(inside, routes.astype(f32), 0.0), axis=0, keepdims=True)
+    )
+    weight = column(jnp.sum(jnp.where(inside, rw_ref[...], 0.0), axis=0, keepdims=True))
     group = jnp.where(chosen == expert.astype(f32), 0.0, 1.0)
-    lane_i = lax.broadcasted_iota(jnp.int32, (token_count, token_count), 1)
-    row_i = lax.broadcasted_iota(jnp.int32, (token_count, token_count), 0)
     lane = lane_i.astype(f32)
     groups = jnp.where(lane == group, has_route, 0.0)
     before = jnp.where(lane_i < row_i, 1.0, 0.0)
@@ -298,7 +323,8 @@
         other[:, cols] = packed[half:]
 
     pl.semaphore_wait(barrier, 11)
-    c0.start()
+    for copy in c0:
+        copy.start()
     c1.start()
     c2.start()
     seg_copies = []
@@ -326,53 +352,65 @@
             rows, wd[:, c * piece : (c + 1) * piece], preferred_element_type=f32
         )
 
-    c1.wait_recv()
-    c5.start()
-    c0.wait_recv()
-    c3.start()
-    c4.start()
+    for b in range(4):
+        c0[b].wait_recv()
+        c3[b].start()
+        c4[b].start()
+        if b == 1:
+            c1.wait_recv()
+            c5.start()
+    for b in range(4):
+        c4[b].wait_recv()
+        c6[b].start()
     for load in loads:
         load.wait()
     rows = expert_rows(0)
     for c in range(CHUNKS):
         own[c] = down(rows, c)
     c2.wait_recv()
-    c4.wait_recv()
-    c6.start()
     rows = expert_rows(2)
     for c in range(CHUNKS):
         pz[c] = down(rows, c).astype(bf16)
         if c < 2:
-            to_z[c].start()
-    c3.wait_recv()
+            to_z[c, 1].start()
+    for copy in c3:
+        copy.wait_recv()
     rows = expert_rows(1)
     for c in (2, 3, 0, 1):
         py[c] = down(rows, c).astype(bf16)
         if c >= 2:
-            to_y[c].start()
+            to_y[c, 1].start()
     c5.wait_recv()
-    c6.wait_recv()
+    for copy in c6:
+        copy.wait_recv()
     rows = expert_rows(3)
-    for c in (0, 2, 1, 3):
-        pd[c] = down(rows, c).astype(bf16)
-        first_hop[c].start()
-    for c in (0, 2, 1, 3):
-        first_hop[c].wait_recv()
-        if c < 2:
-            py[c] = (py[c].astype(f32) + r1[c].astype(f32)).astype(bf16)
-            to_y[c].start()
-        else:
-            pz[c] = (pz[c].astype(f32) + r1[c].astype(f32)).astype(bf16)
-            to_z[c].start()
-    weights.start()
     order = (0, 2, 1, 3)
     for c in order:
-        to_y[c].wait_recv()
-        to_z[c].wait_recv()
-        total = own[c] + r2y[c].astype(f32) + r2z[c].astype(f32)
-        own[c] = total
-        sm[c] = total[half:].astype(bf16)
-        to_mirror[c].start()
+        pd[c] = down(rows, c).astype(bf16)
+        first_hop[c, 1].start()
+    for c in order:
+        first_hop[c, 0].start()
+    for c in order:
+        (to_z if c < 2 else to_y)[c, 0].start()
+    for h in (1, 0):
+        part = slice(h * half, (h + 1) * half)
+        for c in order:
+            first_hop[c, h].wait_recv()
+            out, copies = (py, to_y) if c < 2 else (pz, to_z)
+            out[c, part] = (out[c, part].astype(f32) + r1[c, part].astype(f32)).astype(bf16)
+            copies[c, h].start()
+    weights.start()
+    for h in (1, 0):
+        part = slice(h * half, (h + 1) * half)
+        for c in order:
+            to_y[c, h].wait_recv()
+            to_z[c, h].wait_recv()
+            total = own[c, part] + r2y[c, part].astype(f32) + r2z[c, part].astype(f32)
+            if h:
+                sm[c] = total.astype(bf16)
+                to_mirror[c].start()
+            else:
+                own[c, part] = total
 
     def onward(c):
         return pltpu.make_async_remote_copy(
@@ -403,12 +441,11 @@
 
     for copy in seg_copies:
         copy.wait_recv()
-    mine = segcol_ref[...]
-    start = jnp.sum(
-        jnp.where(segrow_ref[...] < mine, 1.0, 0.0), axis=-1, keepdims=True
-    )
+    own_row = segrow_ref[...].astype(f32)
+    mine = column(own_row)
+    start = jnp.sum(jnp.where(own_row < mine, 1.0, 0.0), axis=-1, keepdims=True)
     for k in range(7):
-        start += jnp.sum(jnp.where(segs[k] < mine, 1.0, 0.0), axis=-1, keepdims=True)
+        start += jnp.sum(jnp.where(segs[k].astype(f32) < mine, 1.0, 0.0), axis=-1, keepdims=True)
     index = (
         lax.broadcasted_iota(jnp.int32, (token_count, 1), 0) + me * token_count
     ).astype(f32)
@@ -423,7 +460,7 @@
     def project(rows):
         result = jnp.dot(rows[:, : piece // 2], wbuf[0], preferred_element_type=f32)
         result += jnp.dot(rows[:, piece // 2 :], wbuf[1], preferred_element_type=f32)
-        return result.astype(bf16)
+        return result
 
     def arrival(source):
         return pltpu.make_async_remote_copy(
@@ -432,27 +469,37 @@
             device_id_type=MESH,
         )
 
-    def partial_copy(k):
-        target = lax.rem(z + k, 4)
+    z_side = z // 2 * 2 + 1 - z % 2
+
+    def partial_copy(slot, target):
         return pltpu.make_async_remote_copy(
-            src_ref=lbuf_out(k), dst_ref=rbuf.at[k - 1], send_sem=p_send.at[k - 1],
-            recv_sem=p_recv.at[k - 1], device_id=(section, target * 2 + y), device_id_type=MESH,
-        )
-
-    def lbuf_out(k):
-        return rbuf.at[2 + k]
-
-    for k in (2, 1, 3):
-        source = lax.rem(z + k, 4)
-        arrival(source).wait_recv()
-        rbuf[2 + k] = project(lbuf[source])
-        partial_copy(k).start()
+            src_ref=rbuf.at[3 + slot], dst_ref=rbuf.at[slot], send_sem=p_send.at[slot],
+            recv_sem=p_recv.at[slot], device_id=(section, target), device_id_type=MESH,
+        )
+
+    partial_copies = [
+        partial_copy(0, z_peer), partial_copy(1, z_peer), partial_copy(2, mirror)
+    ]
+    source = lax.rem(z_side + 2, 4)
+    arrival(source).wait_recv()
+    rbuf[4] = project(lbuf[source]).astype(bf16)
+    partial_copies[1].start()
+    source = lax.rem(z + 2, 4)
+    arrival(source).wait_recv()
+    crossing = project(lbuf[source])
+    arrival(z_side).wait_recv()
+    rbuf[3] = project(lbuf[z_side]).astype(bf16)
+    partial_copies[0].start()
+    partial_copies[1].wait_recv()
+    rbuf[5] = (crossing + rbuf[1].astype(f32)).astype(bf16)
+    partial_copies[2].start()
     arrival(z).wait_recv()
-    mixed = project(lbuf[z]).astype(f32)
+    mixed = project(lbuf[z])
     scale_copy.wait_recv()
-    for k in range(1, 4):
-        partial_copy(k).wait_recv()
-        mixed += rbuf[k - 1].astype(f32)
+    partial_copies[0].wait_recv()
+    mixed += rbuf[0].astype(f32)
+    partial_copies[2].wait_recv()
+    mixed += rbuf[2].astype(f32)
     mixed *= scale_in[:, 0:1]
 
     def turn(values, gain):
@@ -495,14 +542,15 @@
         out = jnp.dot(probs.astype(bf16), values, preferred_element_type=f32) / mass
         att_ref[:, h * head_dim : (h + 1) * head_dim] = out.astype(bf16)
 
-    for copy in [c0, c1, c2, c3, c4, c5, c6, weights, scale_copy]:
+    for copy in [c1, c2, c5, weights, scale_copy, *c0, *c3, *c4, *c6]:
         copy.wait_send()
-    for copy in first_hop + to_y + to_z + to_mirror + seg_copies + kv_copies:
+    for copies in (first_hop, to_y, to_z):
+        for copy in copies.values():
+            copy.wait_send()
+    for copy in to_mirror + seg_copies + kv_copies + partial_copies:
         copy.wait_send()
     for c in range(CHUNKS):
         onward(c).wait_send()
-    for k in range(1, 4):
-        partial_copy(k).wait_send()
 
 
 def fused_on_device(
@@ -529,7 +577,7 @@
             jax.ShapeDtypeStruct((token_count, width), bf16),
             jax.ShapeDtypeStruct((token_count, w_query.shape[-1]), bf16),
         ),
-        in_specs=[vmem] * 3 + [hbm] * 5 + [vmem] * 5,
+        in_specs=[vmem] * 3 + [hbm] * 5 + [vmem] * 4,
         out_specs=(vmem, vmem),
         scratch_shapes=[
             pltpu.VMEM((4, token_count, width), bf16),
@@ -556,7 +604,7 @@
             pltpu.VMEM((7, 1, token_count), jnp.int32),
             pltpu.VMEM((token_count, token_count), bf16),
             dma((16,)),
-            dma((25,)), dma((25,)),
+            dma((67,)), dma((67,)),
             dma((4,)), dma((4,)),
             dma((3,)), dma((3,)),
             dma((reach,)), dma((reach,)),
@@ -566,9 +614,9 @@
             collective_id=0, has_side_effects=True, vmem_limit_bytes=56 * 1024 * 1024
         ),
     )(
-        tokens[0], routes[0], router_weights[0], w_gate[0, 0], w_up[0, 0], w_down[0, 0],
+        tokens[0], routes[0].T, router_weights[0].T, w_gate[0, 0], w_up[0, 0], w_down[0, 0],
         w_query[0], w_keyval[0], gain_query, gain_key, segment_ids,
-        segment_ids.reshape(token_count, 1), frequency,
+        frequency,
     )
     return (layer_out[None], attended[None])
 

time: 192 us -> 172 us (0.90)
  Pallas kernels: 183 us -> 165 us
  local copies, waits for them, and re-layouts: 8.17 us -> 3.96 us
    pallas_call x1, Pallas kernels: 183 us -> 165 us  [fused_on_device(): pl.pallas_call(fused_kernel, out_shape=(jax.ShapeDtypeStruct((token_count...]
    unnamed x4 -> x2, local copies, waits for them, and re-layouts: 6.79 us -> 3.96 us
where the time goes in v2:
time: 172 us; the launch traced here: 170 us
  Pallas kernels  165 us (96%)
  local copies, waits for them, and re-layouts  3.96 us (2%)
    pallas_call x1, Pallas kernels, fused_on_device(): pl.pallas_call(fused_kernel, out_shape=(jax.ShapeDtypeStruct((token_count...  165 us
    unnamed x2, local copies, waits for them, and re-layouts  3.96 us

profile of v2, /device:TPU:7, one launch (start us, length us, event | category | flops | bytes accessed | tf_op | source)
XLA Modules:
  0.0 170.3 jit_solution(6840565821841762398)
XLA Ops:
  0.6 0.6 maximum_bitcast_fusion.freq_ref
  1.2 165.1 %shard_map.122 = (bf16[128,4096]{1,0:T(8,128)(2,1)}, bf16[128,1024]{1,0:T(8,128)(2,1)}) custom-call(bf16[128,4096]{1,0:T(8,128)(2,1)} %bitcast.20, s32[8,128]{1,0:T(8,128)} %bitcast.24, f32[8,128]{1,0:T(8,128)} %bitcast.25, bf16[4096,384]{1,0:T(8,128)(2,1)} %bitcast.16, bf16[4096,384]{1,0:T(8,128)(2,1)} %bitcast.17, bf16[384,4096]{1,0:T(8,128)(2,1)} %bitcast.18, ...), custom_call_target="tpu_custom_call" | custom-call | tf_op jit(solution)/shard_map/pallas_call | solution.py:574
  166.3 2.3 %copy.15 = bf16[1,128,4096]{2,1,0:T(8,128)(2,1)} copy(bf16[1,128,4096]{2,1,0:T(8,128)(2,1)} %bitcast.19) | data formatting | bytes 2097152
  168.6 1.7 copy.16
  (1 shorter events, 0.0 us)

commit v3 on v2

--- a/solution.py
+++ b/solution.py
@@ -269,7 +269,9 @@
     c2 = remote(xbuf.at[0, low], xbuf.at[2, low], 2, z_peer)
     c3 = [remote(xbuf.at[0, u], xbuf.at[1, u], 31 + b, y_peer) for b, u in enumerate(upper)]
     c4 = [remote(xbuf.at[0, u], xbuf.at[2, u], 35 + b, z_peer) for b, u in enumerate(upper)]
-    c5 = remote(xbuf.at[1, low], xbuf.at[3, low], 5, z_peer)
+    first, second = pl.ds(0, half // 2), pl.ds(half // 2, half // 2)
+    c5 = remote(xbuf.at[1, first], xbuf.at[3, first], 5, z_peer)
+    c7 = remote(xbuf.at[2, second], xbuf.at[3, second], 6, y_peer)
     c6 = [remote(xbuf.at[2, u], xbuf.at[3, u], 39 + b, y_peer) for b, u in enumerate(upper)]
     def parts(src, dst, base, target):
         return {
@@ -359,6 +361,8 @@
         if b == 1:
             c1.wait_recv()
             c5.start()
+            c2.wait_recv()
+            c7.start()
     for b in range(4):
         c4[b].wait_recv()
         c6[b].start()
@@ -367,7 +371,6 @@
     rows = expert_rows(0)
     for c in range(CHUNKS):
         own[c] = down(rows, c)
-    c2.wait_recv()
     rows = expert_rows(2)
     for c in range(CHUNKS):
         pz[c] = down(rows, c).astype(bf16)
@@ -381,6 +384,7 @@
         if c >= 2:
             to_y[c, 1].start()
     c5.wait_recv()
+    c7.wait_recv()
     for copy in c6:
         copy.wait_recv()
     rows = expert_rows(3)
@@ -471,34 +475,41 @@
 
     z_side = z // 2 * 2 + 1 - z % 2
 
-    def partial_copy(slot, target):
+    def partial_copy(slot, h, target):
+        rows = pl.ds(h * half, half)
         return pltpu.make_async_remote_copy(
-            src_ref=rbuf.at[3 + slot], dst_ref=rbuf.at[slot], send_sem=p_send.at[slot],
-            recv_sem=p_recv.at[slot], device_id=(section, target), device_id_type=MESH,
-        )
-
-    partial_copies = [
-        partial_copy(0, z_peer), partial_copy(1, z_peer), partial_copy(2, mirror)
-    ]
+            src_ref=rbuf.at[3 + slot, rows], dst_ref=rbuf.at[slot, rows],
+            send_sem=p_send.at[2 * slot + h], recv_sem=p_recv.at[2 * slot + h],
+            device_id=(section, target), device_id_type=MESH,
+        )
+
+    targets = (z_peer, z_peer, mirror)
+    partial_copies = [[partial_copy(i, h, targets[i]) for h in range(2)] for i in range(3)]
     source = lax.rem(z_side + 2, 4)
     arrival(source).wait_recv()
     rbuf[4] = project(lbuf[source]).astype(bf16)
-    partial_copies[1].start()
+    for copy in partial_copies[1]:
+        copy.start()
     source = lax.rem(z + 2, 4)
     arrival(source).wait_recv()
     crossing = project(lbuf[source])
     arrival(z_side).wait_recv()
     rbuf[3] = project(lbuf[z_side]).astype(bf16)
-    partial_copies[0].start()
-    partial_copies[1].wait_recv()
-    rbuf[5] = (crossing + rbuf[1].astype(f32)).astype(bf16)
-    partial_copies[2].start()
+    for copy in partial_copies[0]:
+        copy.start()
+    for h in range(2):
+        part = slice(h * half, (h + 1) * half)
+        partial_copies[1][h].wait_recv()
+        rbuf[5, part] = (crossing[part] + rbuf[1, part].astype(f32)).astype(bf16)
+        partial_copies[2][h].start()
     arrival(z).wait_recv()
     mixed = project(lbuf[z])
     scale_copy.wait_recv()
-    partial_copies[0].wait_recv()
+    for copy in partial_copies[0]:
+        copy.wait_recv()
     mixed += rbuf[0].astype(f32)
-    partial_copies[2].wait_recv()
+    for copy in partial_copies[2]:
+        copy.wait_recv()
     mixed += rbuf[2].astype(f32)
     mixed *= scale_in[:, 0:1]
 
@@ -542,12 +553,12 @@
         out = jnp.dot(probs.astype(bf16), values, preferred_element_type=f32) / mass
         att_ref[:, h * head_dim : (h + 1) * head_dim] = out.astype(bf16)
 
-    for copy in [c1, c2, c5, weights, scale_copy, *c0, *c3, *c4, *c6]:
+    for copy in [c1, c2, c5, c7, weights, scale_copy, *c0, *c3, *c4, *c6]:
         copy.wait_send()
     for copies in (first_hop, to_y, to_z):
         for copy in copies.values():
             copy.wait_send()
-    for copy in to_mirror + seg_copies + kv_copies + partial_copies:
+    for copy in to_mirror + seg_copies + kv_copies + sum(partial_copies, []):
         copy.wait_send()
     for c in range(CHUNKS):
         onward(c).wait_send()
@@ -606,7 +617,7 @@
             dma((16,)),
             dma((67,)), dma((67,)),
             dma((4,)), dma((4,)),
-            dma((3,)), dma((3,)),
+            dma((6,)), dma((6,)),
             dma((reach,)), dma((reach,)),
             dma((7,)), dma((7,)),
         ],

time: 172 us -> 164 us (0.953)
  Pallas kernels: 165 us -> 158 us
    pallas_call x1, Pallas kernels: 165 us -> 158 us  [fused_on_device(): pl.pallas_call(fused_kernel, out_shape=(jax.ShapeDtypeStruct((token_count...]
where the time goes in v3:
time: 164 us
  Pallas kernels  158 us (96%)
  local copies, waits for them, and re-layouts  3.96 us (2%)
    pallas_call x1, Pallas kernels, fused_on_device(): pl.pallas_call(fused_kernel, out_shape=(jax.ShapeDtypeStruct((token_count...  158 us
    unnamed x2, local copies, waits for them, and re-layouts  3.96 us

profile of v3, /device:TPU:7, one launch (start us, length us, event | category | flops | bytes accessed | tf_op | source)
XLA Modules:
  0.0 163.6 jit_solution(7802236514549684135)
XLA Ops:
  0.6 0.6 maximum_bitcast_fusion.freq_ref
  1.2 158.4 %shard_map.122 = (bf16[128,4096]{1,0:T(8,128)(2,1)}, bf16[128,1024]{1,0:T(8,128)(2,1)}) custom-call(bf16[128,4096]{1,0:T(8,128)(2,1)} %bitcast.20, s32[8,128]{1,0:T(8,128)} %bitcast.24, f32[8,128]{1,0:T(8,128)} %bitcast.25, bf16[4096,384]{1,0:T(8,128)(2,1)} %bitcast.16, bf16[4096,384]{1,0:T(8,128)(2,1)} %bitcast.17, bf16[384,4096]{1,0:T(8,128)(2,1)} %bitcast.18, ...), custom_call_target="tpu_custom_call" | custom-call | tf_op jit(solution)/shard_map/pallas_call | solution.py:585
  159.6 2.3 %copy.15 = bf16[1,128,4096]{2,1,0:T(8,128)(2,1)} copy(bf16[1,128,4096]{2,1,0:T(8,128)(2,1)} %bitcast.19) | data formatting | bytes 2097152
  161.9 1.7 %copy.16 = bf16[1,128,1024]{2,1,0:T(8,128)(2,1)} copy(bf16[1,128,1024]{2,1,0:T(8,128)(2,1)} %bitcast.23) | data formatting | bytes 524288
  (1 shorter events, 0.0 us)
